TPU v7x, 32 devices: a whole 2x2x4 slice. The times are simulated.
32 devices in a mesh: slab: 16 (over z, y, core), batch: 2 (over x).
Axes of the slice: x: 2, y: 2, z: 4, core: 2. Of those that a mesh axis runs over, the one named last changes fastest.
Arguments:
- features: float32 [2, 20, 64, 128, 128], P('batch', None, 'slab'), may hold values from -6 to 6
- cotangent: bfloat16 [2, 20, 64, 128, 128], P('batch', None, 'slab'), may hold values from -6 to 6
- spectral_weight: bfloat16 [768, 9600], P('slab'), may hold values from -6 to 6
- pointwise_weight: float32 [20, 20], replicated, may hold values from -1.25 to 1.25
Outputs:
- grad_features: bfloat16 [2, 20, 64, 128, 128], P('batch', None, 'slab')
- grad_spectral: float32 [768, 9600], P('slab')
All inputs are finite; a program needn't handle non-finite values.
Results may differ from a plain program's by a relative error of at most 0.001.
Values sent between devices are 32-bit elements; how exact they have to be, the bound alone decides.
A program may use at most 128 MiB of HBM per device.

v0:
```python
import functools
import math

import jax
import jax.numpy as jnp
import numpy as np
from jax import lax
from jax.experimental import pallas as pl
from jax.experimental.pallas import tpu as pltpu
from jax.sharding import PartitionSpec as P

KX = 12
KY = 12
PAD = 16
HALF = KX // 2
TERMS = KX + 1
ROWS = 16

f32 = jnp.float32
bf16 = jnp.bfloat16


def angles(count, length):
    steps = np.arange(count)
    signed = np.where(steps < count // 2, steps, steps - count)
    turns = np.mod(signed[:, None] * np.arange(length)[None, :], length)
    return turns * (2.0 * math.pi / length)


def halves(value):
    high = value.astype(bf16)
    return high, (value - high.astype(f32)).astype(bf16)


def np_halves(value):
    value = np.asarray(value, np.float32)
    high = value.astype(jnp.bfloat16)
    return high, (value - high.astype(np.float32)).astype(jnp.bfloat16)


def padded(table, rows):
    return np.concatenate([table, np.zeros((rows - table.shape[0], table.shape[1]))], 0)


def forward_table(length):
    angle = angles(KY, length)
    both = np.concatenate([padded(np.cos(angle), PAD), padded(np.sin(angle), PAD)], 0)
    high, low = np_halves(both)
    top = np.concatenate([high, high], 1)
    bottom = np.concatenate([low, np.zeros_like(low)], 1)
    return np.concatenate([top, bottom], 0)


def backward_table(length):
    angle = angles(KY, length)
    both = np.concatenate([padded(np.cos(angle), PAD), padded(np.sin(angle), PAD)], 0).T
    high, low = np_halves(both)
    return np.concatenate([high, high, low], 1)


def plane_terms(length):
    turns = np.mod(np.arange(HALF + 1)[:, None] * np.arange(length)[None, :], length)
    angle = turns * (2.0 * math.pi / length)
    return np.concatenate([np.cos(angle), np.sin(angle)[1:]], 0).astype(np.float32).reshape(-1)


def spread_table(channels, width):
    table = np.zeros((2 * channels, 2 * width), np.float32)
    for c in range(channels):
        for o in range(channels):
            table[c, c * channels + o] = 1.0
            table[channels + o, width + c * channels + o] = 1.0
    return np.concatenate([table, table], 0).astype(jnp.bfloat16)


def collect_table(channels, rows, width):
    table = np.zeros((rows, width), np.float32)
    for c in range(channels):
        table[c, c * channels : (c + 1) * channels] = 1.0
    return table.astype(jnp.bfloat16)


def swap(value, owned):
    lane = lax.broadcasted_iota(jnp.int32, value.shape, 1)
    up = pltpu.roll(value, owned, 1)
    down = pltpu.roll(value, 128 - owned, 1)
    return jnp.where(lane < owned, down, jnp.where(lane < 2 * owned, -up, 0.0))


def pieces(owner, owned, depth):
    out = []
    mode = owner * owned
    while mode < (owner + 1) * owned:
        a, j = divmod(mode, depth)
        count = min(depth - j, (owner + 1) * owned - mode)
        out.append((mode - owner * owned, a, j, count))
        mode += count
    return out


def shifted(value, amount):
    amount %= 128
    return value if amount == 0 else pltpu.roll(value, amount, 1)


def kernel(
    n,
    peers,
    feat_ref,
    cot_ref,
    w_ref,
    kron_ref,
    fwd_ref,
    bwd_ref,
    spread_ref,
    collect_ref,
    plane_ref,
    gf_ref,
    gw_ref,
    lines,
    send,
    recv,
    spec,
    adj,
    send2,
    recv2,
    back,
    point,
    send_sem,
    recv_sem,
    send2_sem,
    recv2_sem,
    spec_send_sem,
    spec_recv_sem,
    local_sem,
):
    channels, planes, length, lanes = feat_ref.shape
    depth = lanes // 2
    owned = w_ref.shape[0]
    both = 2 * channels
    me = lax.axis_index("slab")
    mine = lax.axis_index("batch")
    scale = 1.0 / (planes * n * length)
    pair = 2

    barrier = pltpu.get_barrier_semaphore()

    def greet(step, carry):
        pl.semaphore_signal(
            barrier, inc=1, device_id=(lax.rem(me + step, n), mine), device_id_type=pl.DeviceIdType.MESH
        )
        return carry

    lax.fori_loop(1, n, greet, 0)

    def greet_batch(step, carry):
        pl.semaphore_signal(
            barrier, inc=1, device_id=(me, lax.rem(mine + step, peers)), device_id_type=pl.DeviceIdType.MESH
        )
        return carry

    lax.fori_loop(1, peers, greet_batch, 0)

    lane16 = lax.broadcasted_iota(jnp.int32, (PAD, lanes), 1)
    sign = jnp.where(lane16 < depth, 1.0, -1.0).astype(f32)

    def store_lines(out, row, first, c):
        total = out[: 2 * PAD] + out[2 * PAD :]
        for k in range(pair):
            part = total[:, k * lanes : (k + 1) * lanes]
            value = part[:PAD] + sign * pltpu.roll(part[PAD:], depth, 1)
            if row:
                value = value * scale
            lines[pl.ds((first + k) * both + row * channels + c, PAD, stride=planes * both), :] = value

    def along_y(c, carry):
        for first in range(0, planes, pair):
            block = jnp.concatenate([feat_ref[c, first + k] for k in range(pair)], 1)
            high, low = halves(block)
            out = jnp.dot(
                fwd_ref[...], jnp.concatenate([high, low], 0), preferred_element_type=f32
            )
            store_lines(out, 0, first, c)
            block = jnp.concatenate([cot_ref[c, first + k] for k in range(pair)], 1)
            out = jnp.dot(fwd_ref[:, :length], block, preferred_element_type=f32)
            store_lines(out, 1, first, c)
        return carry

    lax.fori_loop(0, channels, along_y, 0)

    lane8 = lax.broadcasted_iota(jnp.int32, (8, lanes), 1)
    groups = both // 8

    def fetch(x, owner, group):
        value = jnp.zeros((8, lanes), f32)
        for start, a, j, count in pieces(owner, owned, depth):
            row = pl.multiple_of((a * planes + x) * both + group * 8, 8)
            source = lines[pl.ds(row, 8), :]
            for part in range(2):
                at = part * owned + start
                moved = shifted(source, at - (part * depth + j))
                value = jnp.where((lane8 >= at) & (lane8 < at + count), moved, value)
        return value

    room = lanes - 2 * owned

    def pack(x, carry):
        for owner in range(n):
            extra = fetch(x, owner, groups - 1)
            for group in range(groups - 1):
                value = fetch(x, owner, group)
                if group < 3:
                    moved = shifted(extra, 2 * owned - group * room)
                    value = jnp.where(lane8 < 2 * owned, value, moved)
                send[owner, x, group * 8 : group * 8 + 8, :] = value
        return carry

    lax.fori_loop(0, planes, pack, 0)

    pl.semaphore_wait(barrier, n - 1 + peers - 1)

    def first_copy(step):
        other = lax.rem(me + step, n)
        return pltpu.make_async_remote_copy(
            src_ref=send.at[other],
            dst_ref=recv.at[me],
            send_sem=send_sem.at[step],
            recv_sem=recv_sem.at[step],
            device_id=(other, mine),
            device_id_type=pl.DeviceIdType.MESH,
        )

    def start_first(step, carry):
        first_copy(step).start()
        return carry

    lax.fori_loop(1, n, start_first, 0)
    local = pltpu.make_async_copy(send.at[me], recv.at[me], local_sem.at[0])
    local.start()

    tall = channels * ROWS

    def mix_cells(x, carry):
        for block in range(0, length, ROWS):
            value = cot_ref[:, x, block : block + ROWS, :].reshape(tall, lanes)
            out = jnp.dot(kron_ref[...], value, preferred_element_type=f32)
            total = out[:tall] + out[tall:]
            point[:, x, block : block + ROWS, :] = total.reshape(channels, ROWS, lanes)
        return carry

    lax.fori_loop(0, planes, mix_cells, 0)

    local.wait()

    def wait_first(step, carry):
        first_copy(step).wait()
        return carry

    lax.fori_loop(1, n, wait_first, 0)

    total_planes = n * planes
    tall_packed = both - 8
    sums = [[None] * 2 for _ in range(TERMS)]
    for part in range(2):
        rows = slice(part * 16, part * 16 + 16)

        def add_plane(x, carry, rows=rows):
            value = recv[x // planes, lax.rem(x, planes), rows, :]
            return tuple(
                carry[t] + plane_ref[t * total_planes + x] * value for t in range(TERMS)
            )

        got = lax.fori_loop(
            0, total_planes, add_plane, tuple(jnp.zeros((16, lanes), f32) for _ in range(TERMS)), unroll=4
        )
        for t in range(TERMS):
            sums[t][part] = got[t]

    lane_full = lax.broadcasted_iota(jnp.int32, (both, lanes), 1)

    def unpack(t):
        main = jnp.concatenate(sums[t], 0)
        last = jnp.zeros((8, lanes), f32)
        for group in range(3):
            moved = shifted(main[group * 8 : group * 8 + 8], group * room - 2 * owned)
            last = jnp.where((lane8 >= group * room) & (lane8 < (group + 1) * room), moved, last)
        whole = jnp.concatenate([main, last], 0)
        return jnp.where(lane_full < 2 * owned, whole, 0.0)

    for k in range(HALF + 1):
        even = unpack(k)
        if k == 0:
            spec[mine, 0] = even
            continue
        odd = swap(unpack(HALF + k), owned)
        if k < HALF:
            spec[mine, k] = even + odd
        spec[mine, KX - k] = even - odd

    def spec_copy(step):
        other = lax.rem(mine + step, peers)
        return pltpu.make_async_remote_copy(
            src_ref=spec.at[mine],
            dst_ref=spec.at[mine],
            send_sem=spec_send_sem.at[step],
            recv_sem=spec_recv_sem.at[step],
            device_id=(me, other),
            device_id_type=pl.DeviceIdType.MESH,
        )

    for step in range(1, peers):
        spec_copy(step).start()

    square = channels * channels
    width = spread_ref.shape[1] // 2

    def spread(sample, k):
        high, low = halves(jnp.concatenate([spec[sample, k]], 0).T)
        return jnp.dot(
            jnp.concatenate([high, low], 1), spread_ref[...], preferred_element_type=f32
        )

    for k in range(KX):
        wide = spread(mine, k)[:, width : width + square]
        real, imag = wide[:owned], wide[owned : 2 * owned]
        w_real = w_ref[:, k * 2 * square : (k * 2 + 1) * square].astype(f32)
        w_imag = w_ref[:, (k * 2 + 1) * square : (k * 2 + 2) * square].astype(f32)
        mixed = jnp.concatenate(
            [
                real * w_real + imag * w_imag,
                imag * w_real - real * w_imag,
                jnp.zeros((lanes - 2 * owned, square), f32),
            ],
            0,
        )
        out = None
        for part in halves(mixed):
            term = lax.dot_general(
                collect_ref[...], part, (((1,), (1,)), ((), ())), preferred_element_type=f32
            )
            out = term if out is None else out + term
        adj[k] = out

    lane_half = lax.broadcasted_iota(jnp.int32, (16, lanes), 1)
    row_half = lax.broadcasted_iota(jnp.int32, (16, lanes), 0)

    def pack_back(value):
        main = value[:16]
        last = jnp.concatenate([value[16:24], jnp.zeros((8, lanes), f32)], 0)
        for group in range(3):
            moved = shifted(last, 2 * owned - group * room)
            if group:
                moved = pltpu.roll(moved, 4 * group, 0)
            here = (lane_half >= 2 * owned) & (row_half >= 4 * group) & (row_half < 4 * group + 4)
            main = jnp.where(here, moved, main)
        return main

    terms = [pack_back(adj[0])]
    for k in range(1, HALF):
        terms.append(pack_back(adj[k] + adj[KX - k]))
    terms.append(pack_back(adj[HALF]))
    for k in range(1, HALF):
        terms.append(pack_back(swap(adj[KX - k] - adj[k], owned)))
    terms.append(pack_back(swap(adj[HALF], owned)))

    def put_plane(x, carry):
        value = plane_ref[x] * carry[0]
        for t in range(1, TERMS):
            value = value + plane_ref[t * total_planes + x] * carry[t]
        send2[x // planes, lax.rem(x, planes)] = value
        return carry

    lax.fori_loop(0, total_planes, put_plane, tuple(terms), unroll=4)

    def second_copy(step):
        other = lax.rem(me + step, n)
        return pltpu.make_async_remote_copy(
            src_ref=send2.at[other],
            dst_ref=recv2.at[me],
            send_sem=send2_sem.at[step],
            recv_sem=recv2_sem.at[step],
            device_id=(other, mine),
            device_id_type=pl.DeviceIdType.MESH,
        )

    def start_second(step, carry):
        second_copy(step).start()
        return carry

    lax.fori_loop(1, n, start_second, 0)
    local2 = pltpu.make_async_copy(send2.at[me], recv2.at[me], local_sem.at[1])
    local2.start()

    for step in range(1, peers):
        spec_copy(step).wait()

    for k in range(KX):
        out_real = out_imag = None
        for sample in range(peers):
            wide = spread(sample, k)
            s_real, s_imag = wide[:owned, :square], wide[owned : 2 * owned, :square]
            g_real = wide[:owned, width : width + square]
            g_imag = wide[owned : 2 * owned, width : width + square]
            t_real = s_real * g_real + s_imag * g_imag
            t_imag = s_real * g_imag - s_imag * g_real
            out_real = t_real if out_real is None else out_real + t_real
            out_imag = t_imag if out_imag is None else out_imag + t_imag
        gw_ref[:, k * 2 * square : (k * 2 + 1) * square] = out_real
        gw_ref[:, (k * 2 + 1) * square : (k * 2 + 2) * square] = out_imag

    local2.wait()

    def wait_second(step, carry):
        second_copy(step).wait()
        return carry

    lax.fori_loop(1, n, wait_second, 0)

    tail = 24

    def unpack_back(x, carry):
        wholes = {}
        for owner in range(n):
            main = recv2[owner, x]
            last = jnp.zeros((16, lanes), f32)
            for group in range(3):
                moved = shifted(main, group * room - 2 * owned)
                if group:
                    moved = pltpu.roll(moved, 16 - 4 * group, 0)
                here = (lane_half >= group * room) & (lane_half < (group + 1) * room)
                last = jnp.where(here, moved, last)
            wholes[owner] = (main[:8], main[8:16], last[:8])
            for a in range(KY):
                first = a * depth // owned
                final = ((a + 1) * depth - 1) // owned
                if final != owner:
                    continue
                for group in range(3):
                    value = jnp.zeros((8, lanes), f32)
                    for source in range(first, final + 1):
                        for start, row, j, count in pieces(source, owned, depth):
                            if row != a:
                                continue
                            for part in range(2):
                                at = part * depth + j
                                moved = shifted(wholes[source][group], at - (part * owned + start))
                                value = jnp.where(
                                    (lane8 >= at) & (lane8 < at + count), moved, value
                                )
                    place = pl.multiple_of((a * planes + x) * tail + group * 8, 8)
                    back[pl.ds(place, 8), :] = value
        for a in range(KY, PAD):
            for group in range(3):
                place = pl.multiple_of((a * planes + x) * tail + group * 8, 8)
                back[pl.ds(place, 8), :] = jnp.zeros((8, lanes), f32)
        return carry

    lax.fori_loop(0, planes, unpack_back, 0)

    def finish(c, carry):
        for first in range(0, planes, pair):
            blocks = []
            for k in range(pair):
                value = back[pl.ds((first + k) * tail + c, PAD, stride=planes * tail), :]
                turned = -sign * pltpu.roll(value, depth, 1)
                blocks.append(jnp.concatenate([value, turned], 0))
            high, low = halves(jnp.concatenate(blocks, 1))
            out = jnp.dot(
                bwd_ref[...], jnp.concatenate([high, low, high], 0), preferred_element_type=f32
            )
            for k in range(pair):
                gf_ref[c, first + k] = (
                    point[c, first + k] + out[:, k * lanes : (k + 1) * lanes]
                ).astype(bf16)
        return carry

    lax.fori_loop(0, channels, finish, 0)


def shards(features, cotangent, spectral_weight, pointwise_weight):
    _, channels, planes, length, lanes = features.shape
    owned = spectral_weight.shape[0]
    n = lax.axis_size("slab")
    peers = lax.axis_size("batch")
    both = 2 * channels
    square = channels * channels
    width = -(-square // 128) * 128
    high = lax.reduce_precision(pointwise_weight.T, 8, 7)
    parts = jnp.concatenate([high, pointwise_weight.T - high], 0)
    kron = jnp.kron(parts, jnp.eye(ROWS, dtype=f32)).astype(bf16)
    vmem = pl.BlockSpec(memory_space=pltpu.VMEM)
    grad_features, grad_spectral = pl.pallas_call(
        functools.partial(kernel, n, peers),
        out_shape=(
            jax.ShapeDtypeStruct(features.shape[1:], bf16),
            jax.ShapeDtypeStruct(spectral_weight.shape, f32),
        ),
        in_specs=[vmem] * 8 + [pl.BlockSpec(memory_space=pltpu.SMEM)],
        out_specs=(vmem, vmem),
        scratch_shapes=[
            pltpu.VMEM((PAD * planes * both, lanes), f32),
            pltpu.VMEM((n, planes, both - 8, lanes), f32),
            pltpu.VMEM((n, planes, both - 8, lanes), f32),
            pltpu.VMEM((peers, KX, both, lanes), f32),
            pltpu.VMEM((KX, 24, lanes), f32),
            pltpu.VMEM((n, planes, 16, lanes), f32),
            pltpu.VMEM((n, planes, 16, lanes), f32),
            pltpu.VMEM((PAD * planes * 24, lanes), f32),
            pltpu.VMEM((channels, planes, length, lanes), f32),
            pltpu.SemaphoreType.DMA((n,)),
            pltpu.SemaphoreType.DMA((n,)),
            pltpu.SemaphoreType.DMA((n,)),
            pltpu.SemaphoreType.DMA((n,)),
            pltpu.SemaphoreType.DMA((peers,)),
            pltpu.SemaphoreType.DMA((peers,)),
            pltpu.SemaphoreType.DMA((2,)),
        ],
        compiler_params=pltpu.CompilerParams(
            collective_id=0, has_side_effects=True, vmem_limit_bytes=58 * 1024 * 1024
        ),
    )(
        features[0],
        cotangent[0],
        spectral_weight,
        kron,
        jnp.asarray(forward_table(length)),
        jnp.asarray(backward_table(length)),
        jnp.asarray(spread_table(channels, width)),
        jnp.asarray(collect_table(channels, 24, square)),
        jnp.asarray(plane_terms(planes * n)),
    )
    return grad_features[None], grad_spectral


def solution(mesh):
    placed = (
        P("batch", None, "slab", None, None),
        P("batch", None, "slab", None, None),
        P("slab", None),
        P(),
    )
    return jax.shard_map(
        shards,
        mesh=mesh,
        in_specs=placed,
        out_specs=(P("batch", None, "slab", None, None), P("slab", None)),
        check_vma=False,
    )
```

profile of v0, /device:TPU:13, one launch (start us, length us, event | category | flops | bytes accessed | tf_op | source)
XLA Modules:
  0.0 75.5 jit_solution(7885182637635370437)
XLA Ops:
  0.6 0.7 bitcast_reduce-precision_fusion
  1.4 0.1 pad_maximum_fusion
  1.4 0.6 multiply_convert_fusion
  2.0 2.8 %convert_element_type.14 = bf16[640,320]{0,1:T(8,128)(2,1)} reshape(bf16[40,16,20,16]{1,0,3,2:T(8,128)(2,1)S(1)} %multiply_convert_fusion) | data formatting | bytes 819200 | tf_op jit(solution)/shard_map/convert_element_type | solution.py:490
  4.9 2.0 %copy.12.kron_ref = bf16[640,320]{1,0:T(8,128)(2,1)} copy(bf16[640,320]{0,1:T(8,128)(2,1)} %convert_element_type.14) | data formatting | bytes 819200 | tf_op jit(solution)/shard_map/convert_element_type | solution.py:490
  6.9 63.7 %shard_map.104 = (bf16[20,4,128,128]{3,2,1,0:T(8,128)(2,1)}, f32[48,9600]{1,0:T(8,128)}) custom-call(f32[20,4,128,128]{3,2,1,0:T(8,128)} %bitcast.12, bf16[20,4,128,128]{3,2,1,0:T(8,128)(2,1)} %bitcast.13, bf16[48,9600]{1,0:T(8,128)(2,1)} %w_ref.1, bf16[640,320]{1,0:T(8,128)(2,1)} %copy.12.kron_ref, bf16[64,256]{1,0:T(8,128)(2,1)} %constant.10.clone.fwd_ref, ...), custom_call_target="tpu_custom_call" | custom-call | tf_op jit(solution)/shard_map/pallas_call | solution.py:492
  70.6 0.0 copy-start
  70.6 3.7 %copy.15 = bf16[1,20,4,128,128]{4,3,2,1,0:T(8,128)(2,1)} copy(bf16[1,20,4,128,128]{4,3,2,1,0:T(8,128)(2,1)} %bitcast.14) | data formatting | bytes 5242880
  74.3 0.0 copy-done
  74.3 1.2 %copy.16 = f32[48,9600]{1,0:T(8,128)} copy(f32[48,9600]{1,0:T(8,128)S(1)} %copy-done) | data formatting | bytes 3686400
  (1 shorter events, 0.0 us)
Async XLA Ops:
  70.6 3.7 %copy-start = (f32[48,9600]{1,0:T(8,128)S(1)}, f32[48,9600]{1,0:T(8,128)}, u32[]{:S(2)}) copy-start(f32[48,9600]{1,0:T(8,128)} %get-tuple-element.11) | copy-start | bytes 5529604
where the time goes:
time: 76 us; the launch traced here: 75.5 us
  Pallas kernels  63.7 us (84%)
  local copies, waits for them, and re-layouts  9.75 us (13%)
  other arithmetic  1.39 us (2%)
    pallas_call x1, Pallas kernels, shards(): pl.pallas_call(functools.partial(kernel, n, peers), out_shape=(jax.ShapeD...  63.7 us
    unnamed x4, local copies, waits for them, and re-layouts  4.93 us
    convert_element_type x2, local copies, waits for them, and re-layouts, shards(): kron = jnp.kron(parts, jnp.eye(ROWS, dtype=f32)).astype(bf16)  4.82 us

commit v1 on v0

--- a/solution.py
+++ b/solution.py
@@ -64,13 +64,13 @@
     return np.concatenate([np.cos(angle), np.sin(angle)[1:]], 0).astype(np.float32).reshape(-1)
 
 
-def spread_table(channels, width):
-    table = np.zeros((2 * channels, 2 * width), np.float32)
+def spread_tables(channels, rows, width):
+    tables = np.zeros((2, rows, width), np.float32)
     for c in range(channels):
         for o in range(channels):
-            table[c, c * channels + o] = 1.0
-            table[channels + o, width + c * channels + o] = 1.0
-    return np.concatenate([table, table], 0).astype(jnp.bfloat16)
+            tables[0, c, c * channels + o] = 1.0
+            tables[1, o, c * channels + o] = 1.0
+    return np.concatenate([tables, tables], 1).astype(jnp.bfloat16)
 
 
 def collect_table(channels, rows, width):
@@ -109,7 +109,8 @@
     feat_ref,
     cot_ref,
     w_ref,
-    kron_ref,
+    pw_ref,
+    expand_ref,
     fwd_ref,
     bwd_ref,
     spread_ref,
@@ -126,6 +127,7 @@
     recv2,
     back,
     point,
+    kron_ref,
     send_sem,
     recv_sem,
     send2_sem,
@@ -137,7 +139,7 @@
     channels, planes, length, lanes = feat_ref.shape
     depth = lanes // 2
     owned = w_ref.shape[0]
-    both = 2 * channels
+    tail = 24
     me = lax.axis_index("slab")
     mine = lax.axis_index("batch")
     scale = 1.0 / (planes * n * length)
@@ -164,16 +166,16 @@
     lane16 = lax.broadcasted_iota(jnp.int32, (PAD, lanes), 1)
     sign = jnp.where(lane16 < depth, 1.0, -1.0).astype(f32)
 
-    def store_lines(out, row, first, c):
+    def store_lines(out, kind, first, c):
         total = out[: 2 * PAD] + out[2 * PAD :]
         for k in range(pair):
             part = total[:, k * lanes : (k + 1) * lanes]
             value = part[:PAD] + sign * pltpu.roll(part[PAD:], depth, 1)
-            if row:
+            if kind:
                 value = value * scale
-            lines[pl.ds((first + k) * both + row * channels + c, PAD, stride=planes * both), :] = value
-
-    def along_y(c, carry):
+            lines[kind, pl.ds((first + k) * tail + c, PAD, stride=planes * tail), :] = value
+
+    def field_lines(c, carry):
         for first in range(0, planes, pair):
             block = jnp.concatenate([feat_ref[c, first + k] for k in range(pair)], 1)
             high, low = halves(block)
@@ -181,64 +183,110 @@
                 fwd_ref[...], jnp.concatenate([high, low], 0), preferred_element_type=f32
             )
             store_lines(out, 0, first, c)
+        return carry
+
+    def gradient_lines(c, carry):
+        for first in range(0, planes, pair):
             block = jnp.concatenate([cot_ref[c, first + k] for k in range(pair)], 1)
             out = jnp.dot(fwd_ref[:, :length], block, preferred_element_type=f32)
             store_lines(out, 1, first, c)
         return carry
 
-    lax.fori_loop(0, channels, along_y, 0)
-
     lane8 = lax.broadcasted_iota(jnp.int32, (8, lanes), 1)
-    groups = both // 8
-
-    def fetch(x, owner, group):
-        value = jnp.zeros((8, lanes), f32)
-        for start, a, j, count in pieces(owner, owned, depth):
-            row = pl.multiple_of((a * planes + x) * both + group * 8, 8)
-            source = lines[pl.ds(row, 8), :]
-            for part in range(2):
-                at = part * owned + start
-                moved = shifted(source, at - (part * depth + j))
-                value = jnp.where((lane8 >= at) & (lane8 < at + count), moved, value)
-        return value
-
+    row8 = lax.broadcasted_iota(jnp.int32, (8, lanes), 0)
+    lane_half = lax.broadcasted_iota(jnp.int32, (16, lanes), 1)
+    row_half = lax.broadcasted_iota(jnp.int32, (16, lanes), 0)
     room = lanes - 2 * owned
 
-    def pack(x, carry):
-        for owner in range(n):
-            extra = fetch(x, owner, groups - 1)
-            for group in range(groups - 1):
-                value = fetch(x, owner, group)
-                if group < 3:
-                    moved = shifted(extra, 2 * owned - group * room)
-                    value = jnp.where(lane8 < 2 * owned, value, moved)
-                send[owner, x, group * 8 : group * 8 + 8, :] = value
-        return carry
-
-    lax.fori_loop(0, planes, pack, 0)
-
-    pl.semaphore_wait(barrier, n - 1 + peers - 1)
-
-    def first_copy(step):
+    def fold(main, last):
+        last = jnp.concatenate([last, jnp.zeros((8, lanes), f32)], 0)
+        for group in range(3):
+            moved = shifted(last, 2 * owned - group * room)
+            if group:
+                moved = pltpu.roll(moved, 4 * group, 0)
+            here = (lane_half >= 2 * owned) & (row_half >= 4 * group) & (row_half < 4 * group + 4)
+            main = jnp.where(here, moved, main)
+        return main
+
+    def unfold(main):
+        last = jnp.zeros((16, lanes), f32)
+        for group in range(3):
+            moved = shifted(main, group * room - 2 * owned)
+            if group:
+                moved = pltpu.roll(moved, 16 - 4 * group, 0)
+            here = (lane_half >= group * room) & (lane_half < (group + 1) * room)
+            last = jnp.where(here, moved, last)
+        return jnp.where(row8 < 4, last[:8], 0.0)
+
+    def pack_kind(kind):
+        def pack(x, carry):
+            for owner in range(n):
+                values = []
+                for group in range(3):
+                    value = jnp.zeros((8, lanes), f32)
+                    for start, a, j, count in pieces(owner, owned, depth):
+                        row = pl.multiple_of((a * planes + x) * tail + group * 8, 8)
+                        source = lines[kind, pl.ds(row, 8), :]
+                        for part in range(2):
+                            at = part * owned + start
+                            moved = shifted(source, at - (part * depth + j))
+                            value = jnp.where((lane8 >= at) & (lane8 < at + count), moved, value)
+                    values.append(value)
+                send[kind, owner, x] = fold(jnp.concatenate(values[:2], 0), values[2])
+            return carry
+
+        lax.fori_loop(0, planes, pack, 0)
+
+    def first_copy(kind, step):
         other = lax.rem(me + step, n)
         return pltpu.make_async_remote_copy(
-            src_ref=send.at[other],
-            dst_ref=recv.at[me],
-            send_sem=send_sem.at[step],
-            recv_sem=recv_sem.at[step],
+            src_ref=send.at[kind, other],
+            dst_ref=recv.at[kind, me],
+            send_sem=send_sem.at[kind, step],
+            recv_sem=recv_sem.at[kind, step],
             device_id=(other, mine),
             device_id_type=pl.DeviceIdType.MESH,
         )
 
-    def start_first(step, carry):
-        first_copy(step).start()
-        return carry
-
-    lax.fori_loop(1, n, start_first, 0)
-    local = pltpu.make_async_copy(send.at[me], recv.at[me], local_sem.at[0])
-    local.start()
+    def own_copy(kind):
+        return pltpu.make_async_copy(send.at[kind, me], recv.at[kind, me], local_sem.at[kind])
+
+    def start_first(kind):
+        def start(step, carry):
+            first_copy(kind, step).start()
+            return carry
+
+        lax.fori_loop(1, n, start, 0)
+        own_copy(kind).start()
+
+    def wait_first(kind):
+        def wait(step, carry):
+            first_copy(kind, step).wait()
+            return carry
+
+        own_copy(kind).wait()
+        lax.fori_loop(1, n, wait, 0)
+
+    lax.fori_loop(0, channels, gradient_lines, 0)
+    pack_kind(1)
+    pl.semaphore_wait(barrier, n - 1 + peers - 1)
+    start_first(1)
+    lax.fori_loop(0, channels, field_lines, 0)
+    pack_kind(0)
+    start_first(0)
 
     tall = channels * ROWS
+    same = (
+        lax.broadcasted_iota(jnp.int32, (tall, tall), 0)
+        ^ lax.broadcasted_iota(jnp.int32, (tall, tall), 1)
+    ) & (ROWS - 1)
+    across = (((1,), (1,)), ((), ()))
+    for place, part in enumerate(halves(pw_ref[...])):
+        outer = lax.dot_general(expand_ref[...], part, across, preferred_element_type=f32)
+        inner = lax.dot_general(
+            outer.astype(bf16), expand_ref[...], across, preferred_element_type=f32
+        )
+        kron_ref[place * tall : (place + 1) * tall, :] = jnp.where(same == 0, inner, 0.0).astype(bf16)
 
     def mix_cells(x, carry):
         for block in range(0, length, ROWS):
@@ -250,78 +298,58 @@
 
     lax.fori_loop(0, planes, mix_cells, 0)
 
-    local.wait()
-
-    def wait_first(step, carry):
-        first_copy(step).wait()
-        return carry
-
-    lax.fori_loop(1, n, wait_first, 0)
-
     total_planes = n * planes
-    tall_packed = both - 8
-    sums = [[None] * 2 for _ in range(TERMS)]
-    for part in range(2):
-        rows = slice(part * 16, part * 16 + 16)
-
-        def add_plane(x, carry, rows=rows):
-            value = recv[x // planes, lax.rem(x, planes), rows, :]
+
+    def spec_copy(kind, step):
+        other = lax.rem(mine + step, peers)
+        return pltpu.make_async_remote_copy(
+            src_ref=spec.at[mine, kind],
+            dst_ref=spec.at[mine, kind],
+            send_sem=spec_send_sem.at[kind, step],
+            recv_sem=spec_recv_sem.at[kind, step],
+            device_id=(me, other),
+            device_id_type=pl.DeviceIdType.MESH,
+        )
+
+    def along_x(kind):
+        def add_plane(x, carry):
+            value = recv[kind, x // planes, lax.rem(x, planes)]
             return tuple(
                 carry[t] + plane_ref[t * total_planes + x] * value for t in range(TERMS)
             )
 
-        got = lax.fori_loop(
-            0, total_planes, add_plane, tuple(jnp.zeros((16, lanes), f32) for _ in range(TERMS)), unroll=4
-        )
-        for t in range(TERMS):
-            sums[t][part] = got[t]
-
-    lane_full = lax.broadcasted_iota(jnp.int32, (both, lanes), 1)
-
-    def unpack(t):
-        main = jnp.concatenate(sums[t], 0)
-        last = jnp.zeros((8, lanes), f32)
-        for group in range(3):
-            moved = shifted(main[group * 8 : group * 8 + 8], group * room - 2 * owned)
-            last = jnp.where((lane8 >= group * room) & (lane8 < (group + 1) * room), moved, last)
-        whole = jnp.concatenate([main, last], 0)
-        return jnp.where(lane_full < 2 * owned, whole, 0.0)
-
-    for k in range(HALF + 1):
-        even = unpack(k)
-        if k == 0:
-            spec[mine, 0] = even
-            continue
-        odd = swap(unpack(HALF + k), owned)
-        if k < HALF:
-            spec[mine, k] = even + odd
-        spec[mine, KX - k] = even - odd
-
-    def spec_copy(step):
-        other = lax.rem(mine + step, peers)
-        return pltpu.make_async_remote_copy(
-            src_ref=spec.at[mine],
-            dst_ref=spec.at[mine],
-            send_sem=spec_send_sem.at[step],
-            recv_sem=spec_recv_sem.at[step],
-            device_id=(me, other),
-            device_id_type=pl.DeviceIdType.MESH,
-        )
-
-    for step in range(1, peers):
-        spec_copy(step).start()
+        zero = jnp.zeros((16, lanes), f32)
+        sums = lax.fori_loop(0, total_planes, add_plane, (zero,) * TERMS, unroll=4)
+
+        def unpack(t):
+            main = jnp.where(lane_half < 2 * owned, sums[t], 0.0)
+            return jnp.concatenate([main, unfold(sums[t])], 0)
+
+        for k in range(HALF + 1):
+            even = unpack(k)
+            if k == 0:
+                spec[mine, kind, 0] = even
+                continue
+            odd = swap(unpack(HALF + k), owned)
+            if k < HALF:
+                spec[mine, kind, k] = even + odd
+            spec[mine, kind, KX - k] = even - odd
+        for step in range(1, peers):
+            spec_copy(kind, step).start()
+
+    wait_first(1)
+    along_x(1)
 
     square = channels * channels
-    width = spread_ref.shape[1] // 2
-
-    def spread(sample, k):
-        high, low = halves(jnp.concatenate([spec[sample, k]], 0).T)
+
+    def spread(sample, kind, k):
+        high, low = halves(spec[sample, kind, k].T)
         return jnp.dot(
-            jnp.concatenate([high, low], 1), spread_ref[...], preferred_element_type=f32
-        )
+            jnp.concatenate([high, low], 1), spread_ref[kind], preferred_element_type=f32
+        )[:, :square]
 
     for k in range(KX):
-        wide = spread(mine, k)[:, width : width + square]
+        wide = spread(mine, 1, k)
         real, imag = wide[:owned], wide[owned : 2 * owned]
         w_real = w_ref[:, k * 2 * square : (k * 2 + 1) * square].astype(f32)
         w_imag = w_ref[:, (k * 2 + 1) * square : (k * 2 + 2) * square].astype(f32)
@@ -341,19 +369,8 @@
             out = term if out is None else out + term
         adj[k] = out
 
-    lane_half = lax.broadcasted_iota(jnp.int32, (16, lanes), 1)
-    row_half = lax.broadcasted_iota(jnp.int32, (16, lanes), 0)
-
     def pack_back(value):
-        main = value[:16]
-        last = jnp.concatenate([value[16:24], jnp.zeros((8, lanes), f32)], 0)
-        for group in range(3):
-            moved = shifted(last, 2 * owned - group * room)
-            if group:
-                moved = pltpu.roll(moved, 4 * group, 0)
-            here = (lane_half >= 2 * owned) & (row_half >= 4 * group) & (row_half < 4 * group + 4)
-            main = jnp.where(here, moved, main)
-        return main
+        return fold(value[:16], value[16:])
 
     terms = [pack_back(adj[0])]
     for k in range(1, HALF):
@@ -388,19 +405,21 @@
         return carry
 
     lax.fori_loop(1, n, start_second, 0)
-    local2 = pltpu.make_async_copy(send2.at[me], recv2.at[me], local_sem.at[1])
+    local2 = pltpu.make_async_copy(send2.at[me], recv2.at[me], local_sem.at[2])
     local2.start()
 
-    for step in range(1, peers):
-        spec_copy(step).wait()
+    wait_first(0)
+    along_x(0)
+    for kind in range(2):
+        for step in range(1, peers):
+            spec_copy(kind, step).wait()
 
     for k in range(KX):
         out_real = out_imag = None
         for sample in range(peers):
-            wide = spread(sample, k)
-            s_real, s_imag = wide[:owned, :square], wide[owned : 2 * owned, :square]
-            g_real = wide[:owned, width : width + square]
-            g_imag = wide[owned : 2 * owned, width : width + square]
+            wide, g_wide = spread(sample, 0, k), spread(sample, 1, k)
+            s_real, s_imag = wide[:owned], wide[owned : 2 * owned]
+            g_real, g_imag = g_wide[:owned], g_wide[owned : 2 * owned]
             t_real = s_real * g_real + s_imag * g_imag
             t_imag = s_real * g_imag - s_imag * g_real
             out_real = t_real if out_real is None else out_real + t_real
@@ -416,20 +435,11 @@
 
     lax.fori_loop(1, n, wait_second, 0)
 
-    tail = 24
-
     def unpack_back(x, carry):
         wholes = {}
         for owner in range(n):
             main = recv2[owner, x]
-            last = jnp.zeros((16, lanes), f32)
-            for group in range(3):
-                moved = shifted(main, group * room - 2 * owned)
-                if group:
-                    moved = pltpu.roll(moved, 16 - 4 * group, 0)
-                here = (lane_half >= group * room) & (lane_half < (group + 1) * room)
-                last = jnp.where(here, moved, last)
-            wholes[owner] = (main[:8], main[8:16], last[:8])
+            wholes[owner] = (main[:8], main[8:16], unfold(main))
             for a in range(KY):
                 first = a * depth // owned
                 final = ((a + 1) * depth - 1) // owned
@@ -482,12 +492,9 @@
     owned = spectral_weight.shape[0]
     n = lax.axis_size("slab")
     peers = lax.axis_size("batch")
-    both = 2 * channels
+    tail = 24
     square = channels * channels
     width = -(-square // 128) * 128
-    high = lax.reduce_precision(pointwise_weight.T, 8, 7)
-    parts = jnp.concatenate([high, pointwise_weight.T - high], 0)
-    kron = jnp.kron(parts, jnp.eye(ROWS, dtype=f32)).astype(bf16)
     vmem = pl.BlockSpec(memory_space=pltpu.VMEM)
     grad_features, grad_spectral = pl.pallas_call(
         functools.partial(kernel, n, peers),
@@ -495,25 +502,26 @@
             jax.ShapeDtypeStruct(features.shape[1:], bf16),
             jax.ShapeDtypeStruct(spectral_weight.shape, f32),
         ),
-        in_specs=[vmem] * 8 + [pl.BlockSpec(memory_space=pltpu.SMEM)],
+        in_specs=[vmem] * 9 + [pl.BlockSpec(memory_space=pltpu.SMEM)],
         out_specs=(vmem, vmem),
         scratch_shapes=[
-            pltpu.VMEM((PAD * planes * both, lanes), f32),
-            pltpu.VMEM((n, planes, both - 8, lanes), f32),
-            pltpu.VMEM((n, planes, both - 8, lanes), f32),
-            pltpu.VMEM((peers, KX, both, lanes), f32),
+            pltpu.VMEM((2, PAD * planes * tail, lanes), f32),
+            pltpu.VMEM((2, n, planes, 16, lanes), f32),
+            pltpu.VMEM((2, n, planes, 16, lanes), f32),
+            pltpu.VMEM((peers, 2, KX, tail, lanes), f32),
             pltpu.VMEM((KX, 24, lanes), f32),
             pltpu.VMEM((n, planes, 16, lanes), f32),
             pltpu.VMEM((n, planes, 16, lanes), f32),
             pltpu.VMEM((PAD * planes * 24, lanes), f32),
             pltpu.VMEM((channels, planes, length, lanes), f32),
+            pltpu.VMEM((2 * channels * ROWS, channels * ROWS), bf16),
+            pltpu.SemaphoreType.DMA((2, n)),
+            pltpu.SemaphoreType.DMA((2, n)),
             pltpu.SemaphoreType.DMA((n,)),
             pltpu.SemaphoreType.DMA((n,)),
-            pltpu.SemaphoreType.DMA((n,)),
-            pltpu.SemaphoreType.DMA((n,)),
-            pltpu.SemaphoreType.DMA((peers,)),
-            pltpu.SemaphoreType.DMA((peers,)),
-            pltpu.SemaphoreType.DMA((2,)),
+            pltpu.SemaphoreType.DMA((2, peers)),
+            pltpu.SemaphoreType.DMA((2, peers)),
+            pltpu.SemaphoreType.DMA((3,)),
         ],
         compiler_params=pltpu.CompilerParams(
             collective_id=0, has_side_effects=True, vmem_limit_bytes=58 * 1024 * 1024
@@ -522,10 +530,11 @@
         features[0],
         cotangent[0],
         spectral_weight,
-        kron,
+        pointwise_weight,
+        jnp.asarray(np.repeat(np.eye(channels), ROWS, 0).astype(jnp.bfloat16)),
         jnp.asarray(forward_table(length)),
         jnp.asarray(backward_table(length)),
-        jnp.asarray(spread_table(channels, width)),
+        jnp.asarray(spread_tables(channels, tail, width)),
         jnp.asarray(collect_table(channels, 24, square)),
         jnp.asarray(plane_terms(planes * n)),
     )

time: 76 us -> 69.4 us (0.913)
  local copies, waits for them, and re-layouts: 9.75 us -> 4.93 us
  other arithmetic: 1.39 us -> 0 us
    convert_element_type x2 -> x0, local copies, waits for them, and re-layouts: 4.82 us -> none  [shards(): kron = jnp.kron(parts, jnp.eye(ROWS, dtype=f32)).astype(bf16)]
where the time goes in v1:
time: 69.4 us; the launch traced here: 69.2 us
  Pallas kernels  63.6 us (92%)
  local copies, waits for them, and re-layouts  4.93 us (7%)
    pallas_call x1, Pallas kernels, shards(): pl.pallas_call(functools.partial(kernel, n, peers), out_shape=(jax.ShapeD...  63.6 us
    unnamed x4, local copies, waits for them, and re-layouts  4.93 us

profile of v1, /device:TPU:13, one launch (start us, length us, event | category | flops | bytes accessed | tf_op | source)
XLA Modules:
  0.0 69.2 jit_solution(14877457217077916803)
XLA Ops:
  0.6 63.6 %shard_map.113 = (bf16[20,4,128,128]{3,2,1,0:T(8,128)(2,1)}, f32[48,9600]{1,0:T(8,128)}) custom-call(f32[20,4,128,128]{3,2,1,0:T(8,128)} %bitcast.3, bf16[20,4,128,128]{3,2,1,0:T(8,128)(2,1)} %bitcast.4, bf16[48,9600]{1,0:T(8,128)(2,1)} %w_ref.1, f32[20,20]{1,0:T(8,128)} %pw_ref.1, bf16[320,20]{1,0:T(8,128)(2,1)} %constant.12.clone.expand_ref, ...), custom_call_target="tpu_custom_call" | custom-call | tf_op jit(solution)/shard_map/pallas_call | solution.py:499
  64.3 0.0 copy-start
  64.3 3.7 %copy.14 = bf16[1,20,4,128,128]{4,3,2,1,0:T(8,128)(2,1)} copy(bf16[1,20,4,128,128]{4,3,2,1,0:T(8,128)(2,1)} %bitcast.5) | data formatting | bytes 5242880
  68.0 0.0 copy-done
  68.0 1.2 %copy.15 = f32[48,9600]{1,0:T(8,128)} copy(f32[48,9600]{1,0:T(8,128)S(1)} %copy-done) | data formatting | bytes 3686400
Async XLA Ops:
  64.3 3.7 %copy-start = (f32[48,9600]{1,0:T(8,128)S(1)}, f32[48,9600]{1,0:T(8,128)}, u32[]{:S(2)}) copy-start(f32[48,9600]{1,0:T(8,128)} %get-tuple-element.9) | copy-start | bytes 5529604

commit v2 on v1

--- a/solution.py
+++ b/solution.py
@@ -106,9 +106,9 @@
 def kernel(
     n,
     peers,
-    feat_ref,
-    cot_ref,
-    w_ref,
+    feat_hbm,
+    cot_hbm,
+    w_hbm,
     pw_ref,
     expand_ref,
     fwd_ref,
@@ -116,6 +116,11 @@
     spread_ref,
     collect_ref,
     plane_ref,
+    gf_hbm,
+    gw_hbm,
+    feat_ref,
+    cot_ref,
+    w_ref,
     gf_ref,
     gw_ref,
     lines,
@@ -135,6 +140,11 @@
     spec_send_sem,
     spec_recv_sem,
     local_sem,
+    cot_sem,
+    feat_sem,
+    w_sem,
+    gf_sem,
+    gw_sem,
 ):
     channels, planes, length, lanes = feat_ref.shape
     depth = lanes // 2
@@ -145,6 +155,15 @@
     scale = 1.0 / (planes * n * length)
     pair = 2
 
+    chunks = cot_sem.shape[0]
+    per = channels // chunks
+
+    def load(source, target, sem, chunk):
+        at = pl.ds(chunk * per, per)
+        return pltpu.make_async_copy(source.at[at], target.at[at], sem.at[chunk])
+
+    for chunk in range(chunks):
+        load(cot_hbm, cot_ref, cot_sem, chunk).start()
     barrier = pltpu.get_barrier_semaphore()
 
     def greet(step, carry):
@@ -267,11 +286,19 @@
         own_copy(kind).wait()
         lax.fori_loop(1, n, wait, 0)
 
-    lax.fori_loop(0, channels, gradient_lines, 0)
+    for chunk in range(chunks):
+        load(feat_hbm, feat_ref, feat_sem, chunk).start()
+    w_copy = pltpu.make_async_copy(w_hbm, w_ref, w_sem.at[0])
+    w_copy.start()
+    for chunk in range(chunks):
+        load(cot_hbm, cot_ref, cot_sem, chunk).wait()
+        lax.fori_loop(chunk * per, (chunk + 1) * per, gradient_lines, 0)
     pack_kind(1)
     pl.semaphore_wait(barrier, n - 1 + peers - 1)
     start_first(1)
-    lax.fori_loop(0, channels, field_lines, 0)
+    for chunk in range(chunks):
+        load(feat_hbm, feat_ref, feat_sem, chunk).wait()
+        lax.fori_loop(chunk * per, (chunk + 1) * per, field_lines, 0)
     pack_kind(0)
     start_first(0)
 
@@ -337,6 +364,7 @@
         for step in range(1, peers):
             spec_copy(kind, step).start()
 
+    w_copy.wait()
     wait_first(1)
     along_x(1)
 
@@ -427,6 +455,8 @@
         gw_ref[:, k * 2 * square : (k * 2 + 1) * square] = out_real
         gw_ref[:, (k * 2 + 1) * square : (k * 2 + 2) * square] = out_imag
 
+    gw_copy = pltpu.make_async_copy(gw_ref, gw_hbm, gw_sem.at[0])
+    gw_copy.start()
     local2.wait()
 
     def wait_second(step, carry):
@@ -467,6 +497,9 @@
 
     lax.fori_loop(0, planes, unpack_back, 0)
 
+    def gf_copy(c):
+        return pltpu.make_async_copy(gf_ref.at[c], gf_hbm.at[c], gf_sem.at[c])
+
     def finish(c, carry):
         for first in range(0, planes, pair):
             blocks = []
@@ -482,9 +515,17 @@
                 gf_ref[c, first + k] = (
                     point[c, first + k] + out[:, k * lanes : (k + 1) * lanes]
                 ).astype(bf16)
+        gf_copy(c).start()
         return carry
 
     lax.fori_loop(0, channels, finish, 0)
+
+    def settle(c, carry):
+        gf_copy(c).wait()
+        return carry
+
+    lax.fori_loop(0, channels, settle, 0)
+    gw_copy.wait()
 
 
 def shards(features, cotangent, spectral_weight, pointwise_weight):
@@ -495,6 +536,7 @@
     tail = 24
     square = channels * channels
     width = -(-square // 128) * 128
+    chunks = math.gcd(channels, 5)
     vmem = pl.BlockSpec(memory_space=pltpu.VMEM)
     grad_features, grad_spectral = pl.pallas_call(
         functools.partial(kernel, n, peers),
@@ -502,9 +544,14 @@
             jax.ShapeDtypeStruct(features.shape[1:], bf16),
             jax.ShapeDtypeStruct(spectral_weight.shape, f32),
         ),
-        in_specs=[vmem] * 9 + [pl.BlockSpec(memory_space=pltpu.SMEM)],
-        out_specs=(vmem, vmem),
+        in_specs=[pl.BlockSpec(memory_space=pl.ANY)] * 3 + [vmem] * 6 + [pl.BlockSpec(memory_space=pltpu.SMEM)],
+        out_specs=(pl.BlockSpec(memory_space=pl.ANY),) * 2,
         scratch_shapes=[
+            pltpu.VMEM(features.shape[1:], f32),
+            pltpu.VMEM(cotangent.shape[1:], bf16),
+            pltpu.VMEM(spectral_weight.shape, bf16),
+            pltpu.VMEM(features.shape[1:], bf16),
+            pltpu.VMEM(spectral_weight.shape, f32),
             pltpu.VMEM((2, PAD * planes * tail, lanes), f32),
             pltpu.VMEM((2, n, planes, 16, lanes), f32),
             pltpu.VMEM((2, n, planes, 16, lanes), f32),
@@ -522,6 +569,11 @@
             pltpu.SemaphoreType.DMA((2, peers)),
             pltpu.SemaphoreType.DMA((2, peers)),
             pltpu.SemaphoreType.DMA((3,)),
+            pltpu.SemaphoreType.DMA((chunks,)),
+            pltpu.SemaphoreType.DMA((chunks,)),
+            pltpu.SemaphoreType.DMA((1,)),
+            pltpu.SemaphoreType.DMA((channels,)),
+            pltpu.SemaphoreType.DMA((1,)),
         ],
         compiler_params=pltpu.CompilerParams(
             collective_id=0, has_side_effects=True, vmem_limit_bytes=58 * 1024 * 1024

time: 69.4 us -> 66.9 us (0.964)
  Pallas kernels: 63.6 us -> 61.1 us
    pallas_call x1, Pallas kernels: 63.6 us -> 61.1 us  [shards(): pl.pallas_call(functools.partial(kernel, n, peers), out_shape=(jax.ShapeD...]
where the time goes in v2:
time: 66.9 us; the launch traced here: 66.7 us
  Pallas kernels  61.1 us (91%)
  local copies, waits for them, and re-layouts  4.93 us (7%)
    pallas_call x1, Pallas kernels, shards(): pl.pallas_call(functools.partial(kernel, n, peers), out_shape=(jax.ShapeD...  61.1 us
    unnamed x4, local copies, waits for them, and re-layouts  4.93 us

profile of v2, /device:TPU:13, one launch (start us, length us, event | category | flops | bytes accessed | tf_op | source)
XLA Modules:
  0.0 66.7 jit_solution(12071435058572694124)
XLA Ops:
  0.6 61.1 %shard_map.113 = (bf16[20,4,128,128]{3,2,1,0:T(8,128)(2,1)}, f32[48,9600]{1,0:T(8,128)}) custom-call(f32[20,4,128,128]{3,2,1,0:T(8,128)} %bitcast.3, bf16[20,4,128,128]{3,2,1,0:T(8,128)(2,1)} %bitcast.4, bf16[48,9600]{1,0:T(8,128)(2,1)} %w_hbm.1, f32[20,20]{1,0:T(8,128)} %pw_ref.1, bf16[320,20]{1,0:T(8,128)(2,1)} %constant.12.clone.expand_ref, ...), custom_call_target="tpu_custom_call" | custom-call | tf_op jit(solution)/shard_map/pallas_call | solution.py:541
  61.8 0.0 copy-start
  61.8 3.7 %copy.14 = bf16[1,20,4,128,128]{4,3,2,1,0:T(8,128)(2,1)} copy(bf16[1,20,4,128,128]{4,3,2,1,0:T(8,128)(2,1)} %bitcast.5) | data formatting | bytes 5242880
  65.5 0.0 copy-done
  65.5 1.2 %copy.15 = f32[48,9600]{1,0:T(8,128)} copy(f32[48,9600]{1,0:T(8,128)S(1)} %copy-done) | data formatting | bytes 3686400
Async XLA Ops:
  61.8 3.7 %copy-start = (f32[48,9600]{1,0:T(8,128)S(1)}, f32[48,9600]{1,0:T(8,128)}, u32[]{:S(2)}) copy-start(f32[48,9600]{1,0:T(8,128)} %get-tuple-element.9) | copy-start | bytes 5529604

commit v3 on v2

--- a/solution.py
+++ b/solution.py
@@ -278,14 +278,6 @@
         lax.fori_loop(1, n, start, 0)
         own_copy(kind).start()
 
-    def wait_first(kind):
-        def wait(step, carry):
-            first_copy(kind, step).wait()
-            return carry
-
-        own_copy(kind).wait()
-        lax.fori_loop(1, n, wait, 0)
-
     for chunk in range(chunks):
         load(feat_hbm, feat_ref, feat_sem, chunk).start()
     w_copy = pltpu.make_async_copy(w_hbm, w_ref, w_sem.at[0])
@@ -339,14 +331,22 @@
         )
 
     def along_x(kind):
-        def add_plane(x, carry):
-            value = recv[kind, x // planes, lax.rem(x, planes)]
-            return tuple(
-                carry[t] + plane_ref[t * total_planes + x] * value for t in range(TERMS)
-            )
-
+        def add_source(source, carry):
+            for plane in range(planes):
+                value = recv[kind, source, plane]
+                at = source * planes + plane
+                carry = tuple(
+                    carry[t] + plane_ref[t * total_planes + at] * value for t in range(TERMS)
+                )
+            return carry
+
+        def add_step(step, carry):
+            first_copy(kind, step).wait()
+            return add_source(lax.rem(me - step + n, n), carry)
+
+        own_copy(kind).wait()
         zero = jnp.zeros((16, lanes), f32)
-        sums = lax.fori_loop(0, total_planes, add_plane, (zero,) * TERMS, unroll=4)
+        sums = lax.fori_loop(1, n, add_step, add_source(me, (zero,) * TERMS))
 
         def unpack(t):
             main = jnp.where(lane_half < 2 * owned, sums[t], 0.0)
@@ -365,7 +365,6 @@
             spec_copy(kind, step).start()
 
     w_copy.wait()
-    wait_first(1)
     along_x(1)
 
     square = channels * channels
@@ -436,7 +435,6 @@
     local2 = pltpu.make_async_copy(send2.at[me], recv2.at[me], local_sem.at[2])
     local2.start()
 
-    wait_first(0)
     along_x(0)
     for kind in range(2):
         for step in range(1, peers):

time: 66.9 us -> 65.7 us (0.982)
  Pallas kernels: 61.1 us -> 59.9 us
    pallas_call x1, Pallas kernels: 61.1 us -> 59.9 us  [shards(): pl.pallas_call(functools.partial(kernel, n, peers), out_shape=(jax.ShapeD...]
where the time goes in v3:
time: 65.7 us; the launch traced here: 65.5 us
  Pallas kernels  59.9 us (91%)
  local copies, waits for them, and re-layouts  4.93 us (8%)
    pallas_call x1, Pallas kernels, shards(): pl.pallas_call(functools.partial(kernel, n, peers), out_shape=(jax.ShapeD...  59.9 us
    unnamed x4, local copies, waits for them, and re-layouts  4.93 us

profile of v3, /device:TPU:13, one launch (start us, length us, event | category | flops | bytes accessed | tf_op | source)
XLA Modules:
  0.0 65.5 jit_solution(637634089024879121)
XLA Ops:
  0.6 59.9 %shard_map.113 = (bf16[20,4,128,128]{3,2,1,0:T(8,128)(2,1)}, f32[48,9600]{1,0:T(8,128)}) custom-call(f32[20,4,128,128]{3,2,1,0:T(8,128)} %bitcast.3, bf16[20,4,128,128]{3,2,1,0:T(8,128)(2,1)} %bitcast.4, bf16[48,9600]{1,0:T(8,128)(2,1)} %w_hbm.1, f32[20,20]{1,0:T(8,128)} %pw_ref.1, bf16[320,20]{1,0:T(8,128)(2,1)} %constant.12.clone.expand_ref, ...), custom_call_target="tpu_custom_call" | custom-call | tf_op jit(solution)/shard_map/pallas_call | solution.py:539
  60.6 0.0 copy-start
  60.6 3.7 %copy.14 = bf16[1,20,4,128,128]{4,3,2,1,0:T(8,128)(2,1)} copy(bf16[1,20,4,128,128]{4,3,2,1,0:T(8,128)(2,1)} %bitcast.5) | data formatting | bytes 5242880
  64.3 0.0 copy-done
  64.3 1.2 %copy.15 = f32[48,9600]{1,0:T(8,128)} copy(f32[48,9600]{1,0:T(8,128)S(1)} %copy-done) | data formatting | bytes 3686400
Async XLA Ops:
  60.6 3.7 %copy-start = (f32[48,9600]{1,0:T(8,128)S(1)}, f32[48,9600]{1,0:T(8,128)}, u32[]{:S(2)}) copy-start(f32[48,9600]{1,0:T(8,128)} %get-tuple-element.9) | copy-start | bytes 5529604
